TPU v7x, 32 devices: a whole 2x2x4 slice. The times are simulated.
32 devices in a mesh: dp: 8 (over y, x, core), expert: 4 (over z).
Axes of the slice: x: 2, y: 2, z: 4, core: 2. Of those that a mesh axis runs over, the one named last changes fastest.
Arguments:
- residual: bfloat16 [512, 4096], P('dp', 'expert'), may hold values from -6 to 6
- queries: bfloat16 [512, 4096], P('dp', 'expert'), may hold values from -25 to 25
- cache_keys: bfloat16 [18432, 1024], P('dp', 'expert'), may hold values from -5 to 5
- cache_values: bfloat16 [18432, 1024], P('dp', 'expert'), may hold values from -18 to 18
- node_of_position: int32 [18432], P('dp'), may hold values from -1 to 20, as said below
- parent: int32 [21], replicated, may hold values from 0 to 4, as said below
- leaf_ids: int32 [512], P('dp'), may hold values from 5 to 20
- routes: int32 [512, 2], P('dp'), may hold values from 0 to 7, all different within a row; in each aligned block of 64 rows (0 to 63, 64 to 127, ...) at most 32 rows name the same one
- gate_weights: bfloat16 [512, 2], P('dp'), may hold values from 0.19921875 to 0.796875
- norm_gain: bfloat16 [4096], replicated, may hold values from 0.5 to 1.5
- w_gate: bfloat16 [8, 4096, 14336], P('expert', None, 'dp'), may hold values from -0.09375 to 0.09375
- w_up: bfloat16 [8, 4096, 14336], P('expert', None, 'dp'), may hold values from -0.09375 to 0.09375
- w_down: bfloat16 [8, 14336, 4096], P('expert', 'dp'), may hold values from -0.046875 to 0.046875
Outputs:
- attention_out: bfloat16 [512, 4096], P('dp', 'expert')
- layer_out: bfloat16 [512, 4096], P('dp', 'expert')
Inputs may be any that keep to these rules, and one draw needn't show every extreme that they name: `node_of_position`: each block of 2304 positions begins with 256 positions of node 0, the root; the rest come in blocks of 128 positions, each holding one non-root node on a leading run of one or more positions and -1 after it; every non-root node holds one or more blocks. Node 0 is the root and its own parent; nodes 1 to 4 have parent 0; the other nodes are leaves with a parent among nodes 1 to 4. `leaf_ids`: every request sits at a leaf. `routes`: the two experts of a request differ; among the 64 requests of one index of dp no expert is named more than 32 times.
All inputs are finite; a program needn't handle non-finite values.
Results may differ from a plain program's by a relative error of at most 0.012.
Values may be sent and summed in bfloat16 or wider, within the bound.
A program may use at most 192 MiB of HBM per device.

v0:
```python
import math

import jax
import jax.numpy as jnp
from jax import lax
from jax.sharding import PartitionSpec as P

Q_HEADS = 32
KV_HEADS = 8
HEAD_DIM = 128
EXPERTS = 8
CAP = 32


eps = 1e-05


def ancestor_nodes(leaf_nodes, parent):
    node_range = jnp.arange(parent.shape[0], dtype=jnp.int32)
    leaf_hot = (leaf_nodes[:, None] == node_range[None, :]).astype(jnp.int32)
    middle = jnp.sum(leaf_hot * parent[None, :], axis=1)
    middle_hot = (middle[:, None] == node_range[None, :]).astype(jnp.int32)
    upper = jnp.sum(middle_hot * parent[None, :], axis=1)
    return jnp.stack([leaf_nodes, middle, upper], axis=1)


def route_matrix(routes, weights, capacity, expert_count):
    row_total = routes.shape[0]
    flat_routes = routes.reshape(-1)
    expert_range = jnp.arange(expert_count, dtype=jnp.int32)
    expert_hot = (flat_routes[:, None] == expert_range[None, :]).astype(jnp.int32)
    slot_ranks = jnp.cumsum(expert_hot, axis=0) - expert_hot
    slot_ids = jnp.sum(slot_ranks * expert_hot, axis=1)
    target = slot_ids * expert_count + flat_routes
    column = jnp.arange(capacity * expert_count, dtype=jnp.int32)
    weighted = (target[:, None] == column[None, :]).astype(jnp.float32) * weights.reshape(-1)[
        :, None
    ].astype(jnp.float32)
    return jnp.sum(weighted.reshape(row_total, 2, capacity * expert_count), axis=1)


def body(
    residual,
    queries,
    cache_keys,
    cache_values,
    node_of_position,
    parent,
    leaf_ids,
    routes,
    gate_weights,
    norm_gain,
    w_gate,
    w_up,
    w_down,
):
    row_count = queries.shape[0]
    feature_count = queries.shape[1]
    dp_ways = lax.axis_size("dp")
    expert_ways = lax.axis_size("expert")
    group_size = Q_HEADS // KV_HEADS
    kv_local = cache_keys.shape[1] // HEAD_DIM
    head_local = kv_local * group_size
    local_experts = w_gate.shape[0]
    model_width = w_down.shape[2]
    capacity = CAP
    score_scale = 1.0 / math.sqrt(HEAD_DIM)
    all_queries, all_leaves, all_routes, all_weights = (
        lax.all_gather(queries, "dp", axis=0, tiled=True),
        lax.all_gather(leaf_ids, "dp", axis=0, tiled=True),
        lax.all_gather(routes, "dp", axis=0, tiled=True),
        lax.all_gather(gate_weights, "dp", axis=0, tiled=True),
    )
    total_rows = all_queries.shape[0]
    block_rows = min(total_rows, 512)
    block_count = total_rows // block_rows
    ancestors = ancestor_nodes(all_leaves, parent).reshape(block_count, block_rows, 3)
    query_blocks = all_queries.reshape(block_count, block_rows, kv_local, group_size, HEAD_DIM)
    key_heads = cache_keys.reshape(-1, kv_local, HEAD_DIM)
    value_heads = cache_values.reshape(-1, kv_local, HEAD_DIM)

    def attend(packed):
        query_block, ancestor_block = packed
        visible = jnp.any(node_of_position[None, :, None] == ancestor_block[:, None, :], axis=2)
        scores = (
            jnp.einsum("tkgd,pkd->tkgp", query_block, key_heads, preferred_element_type=jnp.float32)
            * score_scale
        )
        scores = jnp.where(visible[:, None, None, :], scores, -jnp.inf)
        local_max = jnp.max(scores, axis=3)
        exponent = jnp.exp(scores - local_max[..., None])
        local_total = jnp.sum(exponent, axis=3)
        local_out = jnp.einsum(
            "tkgp,pkd->tkgd",
            exponent.astype(jnp.bfloat16),
            value_heads,
            preferred_element_type=jnp.float32,
        )
        return (local_max, local_total, local_out)

    maxima, totals, outputs = lax.map(attend, (query_blocks, ancestors))
    maxima = maxima.reshape(total_rows, head_local)
    totals = totals.reshape(total_rows, head_local)
    outputs = outputs.reshape(total_rows, head_local * HEAD_DIM)
    got_out, got_max, got_total = (
        lax.all_to_all(outputs, "dp", split_axis=0, concat_axis=0, tiled=True),
        lax.all_to_all(maxima, "dp", split_axis=0, concat_axis=0, tiled=True),
        lax.all_to_all(totals, "dp", split_axis=0, concat_axis=0, tiled=True),
    )
    got_out = got_out.reshape(dp_ways, row_count, head_local, HEAD_DIM)
    got_max = got_max.reshape(dp_ways, row_count, head_local)
    got_total = got_total.reshape(dp_ways, row_count, head_local)
    global_max = jnp.max(got_max, axis=0)
    factor = jnp.exp(got_max - global_max[None])
    attention = (
        jnp.sum(factor[..., None] * got_out, axis=0)
        / jnp.sum(factor * got_total, axis=0)[..., None]
    )
    attention = attention.reshape(row_count, feature_count)
    attention_out = attention.astype(jnp.bfloat16)
    stream = (residual.astype(jnp.float32) + attention).astype(jnp.bfloat16)
    dispatch = route_matrix(routes, jnp.ones_like(gate_weights), capacity, EXPERTS).astype(
        jnp.bfloat16
    )
    slot_data = jnp.einsum(
        "rs,rf->sf", dispatch, stream, preferred_element_type=jnp.float32
    ).astype(jnp.bfloat16)
    slot_data = slot_data.reshape(capacity, EXPERTS, feature_count)
    gain_wide = norm_gain.astype(jnp.float32)
    gathered = lax.all_gather(slot_data, "dp", axis=0, tiled=True)
    rows_wide = lax.all_to_all(gathered, "expert", split_axis=1, concat_axis=2, tiled=True).astype(
        jnp.float32
    )
    inverse = lax.rsqrt(jnp.mean(rows_wide * rows_wide, axis=2, keepdims=True) + eps)
    normed = (rows_wide * inverse * gain_wide).astype(jnp.bfloat16)
    gate_val = jnp.einsum("rxd,xdf->rxf", normed, w_gate, preferred_element_type=jnp.float32)
    up_val = jnp.einsum("rxd,xdf->rxf", normed, w_up, preferred_element_type=jnp.float32)
    hidden = (jax.nn.silu(gate_val) * up_val).astype(jnp.bfloat16)
    expert_y = jnp.einsum("rxf,xfd->rxd", hidden, w_down, preferred_element_type=jnp.float32)
    expert_y = expert_y.reshape(dp_ways, capacity, local_experts, model_width)

    def block_matrix(block_routes, block_weights):
        return route_matrix(block_routes, block_weights, capacity, EXPERTS)

    row_mix = jax.vmap(block_matrix)(
        all_routes.reshape(dp_ways, row_count, 2), all_weights.reshape(dp_ways, row_count, 2)
    )
    row_mix = row_mix.reshape(dp_ways, row_count, capacity, EXPERTS)
    row_mix = lax.dynamic_slice_in_dim(
        row_mix, lax.axis_index("expert") * local_experts, local_experts, 3
    )
    row_mix = row_mix.reshape(dp_ways, row_count, capacity * local_experts)

    def one_pair(pair_index):
        row_block = pair_index // expert_ways
        feature_block = pair_index % expert_ways
        mixing = lax.dynamic_index_in_dim(row_mix, row_block, 0, keepdims=False)
        outs_block = lax.dynamic_index_in_dim(expert_y, row_block, 0, keepdims=False)
        columns = lax.dynamic_slice_in_dim(
            outs_block, feature_block * feature_count, feature_count, 2
        )
        return jnp.dot(
            mixing,
            columns.reshape(capacity * local_experts, feature_count),
            precision=lax.Precision.HIGHEST,
            preferred_element_type=jnp.float32,
        )

    pair_list = jnp.arange(
        row_count * lax.axis_size(("dp", "expert")) // row_count, dtype=jnp.int32
    )
    mixture = lax.psum_scatter(
        lax.map(one_pair, pair_list).reshape(
            row_count * lax.axis_size(("dp", "expert")), feature_count
        ),
        ("dp", "expert"),
        scatter_dimension=0,
        tiled=True,
    )
    layer_out = (stream.astype(jnp.float32) + mixture).astype(jnp.bfloat16)
    return (attention_out, layer_out)


def solution(mesh):
    in_specs = (
        P("dp", "expert"),
        P("dp", "expert"),
        P("dp", "expert"),
        P("dp", "expert"),
        P("dp"),
        P(),
        P("dp"),
        P("dp", None),
        P("dp", None),
        P(),
        P("expert", None, "dp"),
        P("expert", None, "dp"),
        P("expert", "dp", None),
    )
    out_specs = (P("dp", "expert"), P("dp", "expert"))
    return jax.shard_map(body, mesh=mesh, in_specs=in_specs, out_specs=out_specs, check_vma=False)
```

profile of v0, /device:TPU:24, one launch (start us, length us, event | category | flops | bytes accessed | tf_op | source)
XLA Modules:
  0.0 714.8 jit_solution(14726834012590748174)
XLA Ops:
  7.9 1.2 dynamic-slice.7
  10.7 8.0 %all-reduce = s32[512]{0:T(512)S(1)} all-reduce(s32[512]{0:T(512)S(1)} %dynamic-update-slice), channel_id=1, replica_groups=mesh['dp'=8,'expert'=4] {'dp'}, use_global_device_ids=true, to_apply=%add | all-reduce | flops 512 | bytes 4096
  20.2 2.5 compare_reduce_fusion
  22.7 1.8 copy.117
  24.6 2.8 reshape.144
  27.3 7.1 all-gather.5.cloned.1.call-done
  34.4 1.5 copy.118
  35.9 14.1 %fusion.6 = (f32[512,2,4]{0,2,1:T(4,128)S(1)}, f32[2,2304,512,4]{2,1,3,0:T(8,128)}) fusion(pred[512,2304]{0,1:T(8,128)(4,1)S(1)} %copy.117, bf16[512,2,4,128]{0,3,2,1:T(8,128)(2,1)S(1)} %bitcast.128, bf16[2304,2,128,1]{2,1,0,3:T(2,128)(2,1)S(1)} %bitcast.127), kind=kOutput, calls=%fused_computation.10 | convolution fusion | flops 2444226560 | bytes 41172992 | tf_op jit(solution)/shard_map/while/body/eval_jaxpr/tkgd,pkd->tkgp/dot_general | solution.py:86
  50.0 16.0 %fusion.4 = f32[512,2,4]{0,2,1:T(4,128)S(1)} fusion(f32[2,2304,512,4]{2,1,3,0:T(8,128)} %get-tuple-element.168, f32[512,2,4]{0,2,1:T(4,128)S(1)} %get-tuple-element.167, pred[512,2304]{0,1:T(8,128)(4,1)S(1)} %copy.117), kind=kLoop, calls=%fused_computation.8 | loop fusion | flops 37744640 | bytes 38961152 | tf_op jit(solution)/shard_map/while/body/eval_jaxpr/reduce_sum | solution.py:92
  66.8 3.9 all-to-all-start.2
  71.8 3.5 all-to-all-done.2
  75.3 3.5 all-to-all-start
  78.9 16.5 %fusion.14 = f32[512,2,4,128]{3,0,2,1:T(8,128)S(1)} fusion(f32[2,2304,512,4]{2,1,3,0:T(8,128)} %get-tuple-element.168, f32[512,2,4]{0,2,1:T(4,128)S(1)} %get-tuple-element.167, pred[512,2304]{0,1:T(8,128)(4,1)S(1)} %copy.117, bf16[2304,2,128,1]{2,1,0,3:T(2,128)(2,1)S(1)} %bitcast.126), kind=kOutput, calls=%fused_computation.24 | convolution fusion | flops 2453667840 | bytes 42221568 | tf_op jit(solution)/shard_map/while/body/eval_jaxpr/tkgp,pkd->tkgd/dot_general | solution.py:93
  95.4 1.4 copy.125
  96.8 1.9 all_to_all.27
  98.7 4.1 all-to-all-start.1
  104.3 1.4 reduce.7
  106.8 1.9 mul.119
  108.7 2.7 mul.120
  111.5 17.9 %all-to-all-done.1 = f32[8,64,1024]{2,1,0:T(8,128)S(1)} async-done(((f32[8,64,1024]{2,1,0:T(8,128)}), f32[8,64,1024]{2,1,0:T(8,128)S(1)}, u32[]{:S(2)}, u32[]{:S(2)}) %all-to-all-start.1) | async-done | bytes 2097184 | tf_op jit(solution)/shard_map/all_to_all | solution.py:106
  129.4 2.0 multiply_reduce_fusion.1
  132.7 36.0 %all-gather.7.cloned.1.call-done = bf16[256,8,1024]{2,1,0:T(8,128)(2,1)} async-done(((bf16[32,8,1024]{2,1,0:T(8,128)(2,1)}), bf16[256,8,1024]{2,1,0:T(8,128)(2,1)}) %all-gather.7.cloned.1.call-update) | async-done | bytes 4194320 | tf_op jit(solution)/shard_map/all_gather | solution.py:130
  168.6 6.5 copy.137
  175.1 5.3 all-to-all-start.3
  180.5 9.1 %all-gather = s32[8,64,2]{1,2,0:T(2,128)S(1)} all-gather(s32[1,64,2]{1,2,0:T(2,128)S(1)} %bitcast.137), channel_id=1, replica_groups=mesh['dp'=8,'expert'=4] {'dp'}, dimensions={0}, use_global_device_ids=true | all-gather | bytes 4608 | tf_op jit(solution)/shard_map/all_gather | solution.py:71
  189.6 2.5 select_reduce_fusion.1
  192.3 7.8 %all-gather.1 = bf16[8,64,2]{1,2,0:T(2,128)(2,1)S(1)} all-gather(bf16[1,64,2]{1,2,0:T(2,128)(2,1)S(1)} %bitcast.139), channel_id=1, replica_groups=mesh['dp'=8,'expert'=4] {'dp'}, dimensions={0}, use_global_device_ids=true | all-gather | bytes 2304 | tf_op jit(solution)/shard_map/all_gather | solution.py:72
  200.9 71.1 %all-to-all-done.3 = bf16[256,8,1024]{2,0,1:T(8,128)(2,1)} async-done(((bf16[256,8,1024]{2,0,1:T(8,128)(2,1)}), bf16[256,8,1024]{2,0,1:T(8,128)(2,1)}, u32[]{:S(2)}, u32[]{:S(2)}) %all-to-all-start.3) | async-done | bytes 4194336 | tf_op jit(solution)/shard_map/all_to_all | solution.py:131
  272.0 3.2 convert_element_type.99
  275.2 4.1 copy.157
  279.3 3.1 multiply_reduce_fusion
  282.4 20.3 %fusion.21 = f32[2,256,1792]{2,1,0:T(8,128)} fusion(bf16[2,4096,1792]{2,1,0:T(8,128)(2,1)} %param.25, f32[256,2,4096]{2,0,1:T(8,128)} %bitcast.119, f32[4096]{0:T(1024)S(1)} %convert_element_type.92, f32[256,2]{0,1:T(2,128)S(1)} %add_rsqrt_fusion), kind=kOutput, calls=%fused_computation.30 | convolution fusion | flops 7522484224 | bytes 41437184 | tf_op jit(solution)/shard_map/rxd,xdf->rxf/dot_general | solution.py:136
  302.7 35.1 %fusion.32 = f32[2,256,4096]{2,1,0:T(8,128)} fusion(bf16[2,1792,4096]{2,1,0:T(8,128)(2,1)} %param.27, f32[2,256,1792]{2,1,0:T(8,128)} %fusion.21, bf16[2,4096,1792]{2,1,0:T(8,128)(2,1)} %param.26, f32[256,2,4096]{2,0,1:T(8,128)} %bitcast.120, f32[4096]{0:T(1024)S(1)} %convert_element_type.92, f32[256,2]{0,1:T(2,128)S(1)} %add_rsqrt_fusion), kind=kOutput, calls=%fused_computation.66 | convolution fusion | flops 15044182016 | bytes 79185920 | tf_op jit(solution)/shard_map/rxf,xfd->rxd/dot_general | solution.py:139
  337.8 187.1 %while.9 = (s32[]{:T(128)}, f32[32,64,1024]{2,1,0:T(8,128)}, s32[32]{0:T(128)S(1)}, f32[8,64,64]{1,2,0:T(8,128)S(1)}, f32[8,32,2,4096]{3,1,0,2:T(8,128)}, /*inde...) while((s32[]{:T(128)}, f32[32,64,1024]{2,1,0:T(8,128)}, ...), condition=%wide.region_17.18_spmd, body=%wide.region_16.17_spmd.sunk | while | flops 50331676 | bytes 2130904 | solution.py:173
  354.2 1.1 fusion.49
  360.1 1.1 fusion.49
  371.8 1.1 fusion.49
  377.7 1.1 fusion.49
  383.5 1.1 fusion.49
  389.4 1.1 fusion.49
  395.2 1.1 fusion.49
  401.1 1.1 fusion.49
  430.3 1.1 fusion.49
  447.8 1.1 fusion.49
  488.7 1.1 fusion.49
  494.6 1.1 fusion.49
  525.0 181.6 %reduce-scatter.2.cloned.1.call-done = f32[64,1024]{1,0:T(8,128)} async-done(((f32[2048,1024]{1,0:T(8,128)}), f32[64,1024]{1,0:T(8,128)}) %reduce-scatter.2.cloned.1.call-update) | async-done | bytes 262160 | tf_op jit(solution)/shard_map/reduce_scatter | solution.py:172
  706.6 1.7 add_convert_fusion
  (212 shorter events, 98.5 us)
Async XLA Ops:
  7.2 27.2 %all-gather.5.cloned.1.call-start = ((), (), s32[]{:S(2)}) async-start(), calls=%async_computation.5 | async-start | bytes 1179648 | tf_op jit(solution)/shard_map/all_gather | solution.py:69
  50.0 20.7 %copy-start = (bf16[2304,256]{1,0:T(8,128)(2,1)S(1)}, bf16[2304,256]{1,0:T(8,128)(2,1)}, u32[]{:S(2)}) copy-start(bf16[2304,256]{1,0:T(8,128)(2,1)} %param.18) | copy-start | bytes 3538948
  66.8 8.5 %all-to-all-start.2 = ((f32[8,1,512]{2,1,0:T(1,128)}), f32[8,1,512]{2,1,0:T(1,128)}, u32[]{:S(2)}, u32[]{:S(2)}) async-start(f32[8,1,512]{2,1,0:T(1,128)} %reshape.171), calls=%async_computation.2 | async-start | bytes 32768 | tf_op jit(solution)/shard_map/all_to_all | solution.py:108
  75.3 23.3 %all-to-all-start = ((f32[8,1,512]{2,1,0:T(1,128)}), f32[8,1,512]{2,1,0:T(1,128)S(1)}, u32[]{:S(2)}, u32[]{:S(2)}) async-start(f32[8,1,512]{2,1,0:T(1,128)} %reshape.169), calls=%async_computation | async-start | bytes 32768 | tf_op jit(solution)/shard_map/all_to_all | solution.py:107
  95.4 7.4 %copy-start.2 = (s32[64,2]{0,1:T(2,128)S(1)}, s32[64,2]{0,1:T(2,128)}, u32[]{:S(2)}) copy-start(s32[64,2]{0,1:T(2,128)} %param.22) | copy-start | bytes 1540
  98.7 32.8 %copy-start.1 = (bf16[64,1024]{1,0:T(8,128)(2,1)S(1)}, bf16[64,1024]{1,0:T(8,128)(2,1)}, u32[]{:S(2)}) copy-start(bf16[64,1024]{1,0:T(8,128)(2,1)} %param.15) | copy-start | bytes 393220
  98.7 30.7 %all-to-all-start.1 = ((f32[8,64,1024]{2,1,0:T(8,128)}), f32[8,64,1024]{2,1,0:T(8,128)S(1)}, u32[]{:S(2)}, u32[]{:S(2)}) async-start(f32[8,64,1024]{2,1,0:T(8,128)} %all_to_all.27), calls=%async_computation.1 | async-start | bytes 4194304 | tf_op jit(solution)/shard_map/all_to_all | solution.py:106
  102.7 65.9 %all-gather.7.cloned.1.call-start = ((), (), s32[]{:S(2)}) async-start(), calls=%async_computation.6 | async-start | bytes 4718592 | tf_op jit(solution)/shard_map/all_gather | solution.py:130
  132.6 47.8 %copy-start.3 = (bf16[4096]{0:T(1024)(128)(2,1)S(1)}, bf16[4096]{0:T(1024)(128)(2,1)}, u32[]{:S(2)}) copy-start(bf16[4096]{0:T(1024)(128)(2,1)} %param.24) | copy-start | bytes 24580
  132.7 59.6 %copy-start.4 = (bf16[64,2]{0,1:T(2,128)(2,1)S(1)}, bf16[64,2]{0,1:T(2,128)(2,1)}, u32[]{:S(2)}) copy-start(bf16[64,2]{0,1:T(2,128)(2,1)} %param.23) | copy-start | bytes 772
  175.1 96.9 %all-to-all-start.3 = ((bf16[256,8,1024]{2,0,1:T(8,128)(2,1)}), bf16[256,8,1024]{2,0,1:T(8,128)(2,1)}, u32[]{:S(2)}, u32[]{:S(2)}) async-start(bf16[256,8,1024]{2,0,1:T(8,128)(2,1)} %copy.137), calls=%async_computation.3 | async-start | bytes 8388608 | tf_op jit(solution)/shard_map/all_to_all | solution.py:131
  180.4 526.1 %reduce-scatter.2.cloned.1.call-start = ((), (), s32[]{:S(2)}) async-start(), calls=%async_computation.7 | async-start | bytes 8650752 | tf_op jit(solution)/shard_map/reduce_scatter | solution.py:172
Sparse Core Ops, SparseCore 0:
  9.9 24.4 all-gather.4
  132.8 35.8 all-gather.6
  525.1 181.4 reduce-scatter.1
where the time goes:
time: 724 us; the launch traced here: 715 us
  waiting for transfers between devices  318 us (44%)
  matrix products  123 us (17%)
  local copies, waits for them, and re-layouts  96.7 us (13%)
  loops' own time  84.8 us (12%)
  other arithmetic  35.6 us (5%)
  blocking collectives  24.9 us (3%)
  starting transfers between devices  16.9 us (2%)
  between operations  14.7 us (2%)
    reduce_scatter x1, waiting for transfers between devices, body(): lax.psum_scatter(lax.map(one_pair, pair_list).reshape(row_count * lax.axi...  182 us
    another operation x1, loops' own time, body(): lax.map(one_pair, pair_list)  84.8 us
    all_to_all x1, waiting for transfers between devices, body(): lax.all_to_all(gathered, 'expert', split_axis=1, concat_axis=2, tiled=True)  71.1 us
    dynamic_slice x64, local copies, waits for them, and re-layouts, one_pair(): lax.dynamic_slice_in_dim(outs_block, feature_block * feature_count, featu...  41.6 us
    dot_general x32, matrix products, one_pair(): jnp.dot(mixing, columns.reshape(capacity * local_experts, feature_count),...  36.3 us
    all_gather x1, waiting for transfers between devices, body(): gathered = lax.all_gather(slot_data, 'dp', axis=0, tiled=True)  36 us
    dot_general x1, matrix products, body(): jnp.einsum('rxf,xfd->rxd', hidden, w_down, preferred_element_type=jnp.flo...  35.1 us
    dot_general x1, matrix products, body(): jnp.einsum('rxd,xdf->rxf', normed, w_gate, preferred_element_type=jnp.flo...  20.3 us
  transfers between devices with their start and end apart: 7, of which 6 were waited for; matrix products, arithmetic and copies ran while one was open for 6% of the time, Pallas kernels for 0%

commit v1 on v0

v1 whole, which is shorter than its diff:
```python
import functools
import math

import jax
import jax.numpy as jnp
from jax import lax
from jax.experimental import pallas as pl
from jax.experimental.pallas import tpu as pltpu
from jax.sharding import PartitionSpec as P

Q_HEADS = 32
KV_HEADS = 8
HEAD_DIM = 128
EXPERTS = 8
CAP = 32
EPS = 1e-05
HIDE = -1e30
EMPTY = 63
META = 64
MESH = pl.DeviceIdType.MESH
VMEM = pltpu.VMEM


def whole(memory_space=VMEM):
    return pl.BlockSpec(memory_space=memory_space)


def greet(dp_peers, expert_peers):
    barrier = pltpu.get_barrier_semaphore()
    for peer in dp_peers:
        pl.semaphore_signal(barrier, inc=1, device_id={"dp": peer}, device_id_type=MESH)
    for peer in expert_peers:
        pl.semaphore_signal(barrier, inc=1, device_id={"expert": peer}, device_id_type=MESH)
    pl.semaphore_wait(barrier, len(dp_peers) + len(expert_peers))


def remote(src, dst, send, recv, axis, peer):
    return pltpu.make_async_remote_copy(
        src_ref=src, dst_ref=dst, send_sem=send, recv_sem=recv, device_id={axis: peer}, device_id_type=MESH
    )


def attention_kernel(
    n, n_e, kv_local, group,
    qx, keys, values, hot, residual,
    attention_out, gathered, meta,
    qall, so, sl, ro, rl,
    q_send, q_recv, o_send, o_recv, l_send, l_recv, z_send, z_recv, c_send, c_recv, s_send, s_recv,
):
    me, my_e = lax.axis_index("dp"), lax.axis_index("expert")
    rows, features = residual.shape
    half = n // 2
    chip, core = me // 2, me % 2
    sibling = chip * 2 + (1 - core)
    coeff = math.log2(math.e) / math.sqrt(HEAD_DIM)
    greet([(me + j) % n for j in range(1, n)], [(my_e + k) % n_e for k in range(1, n_e)])

    def q_copy(j, slot):
        return remote(qx, qall.at[slot], q_send.at[j], q_recv.at[j], "dp", (me + j) % n)

    for j in range(1, n):
        q_copy(j, me).start()
    qall[me] = qx[...]

    def o_copy(j):
        return remote(so.at[j], ro.at[j], o_send.at[j], o_recv.at[j], "dp", (me + n - j) % n)

    def l_copy(j):
        return remote(sl.at[j], rl.at[j], l_send.at[j], l_recv.at[j], "dp", (me + n - j) % n)

    lane = lax.broadcasted_iota(jnp.int32, (rows, 128), 1)

    def attend(j, carry):
        source = (me + n - j) % n

        @pl.when(j > 0)
        def _():
            q_copy(j, source).wait_recv()

        block = qall[source]
        side = block[:, features:]
        side = jnp.concatenate([side] * group, axis=0)
        logs = jnp.zeros((rows, 128), jnp.float32)
        for kv in range(kv_local):
            first = kv * group
            q = jnp.concatenate(
                [block[:, (first + g) * HEAD_DIM : (first + g + 1) * HEAD_DIM] for g in range(group)], axis=0
            )
            q = jnp.concatenate([q, side], axis=1)
            cut = slice(kv * HEAD_DIM, (kv + 1) * HEAD_DIM)
            k = jnp.concatenate([keys[:, cut], hot[...]], axis=1)
            scores = lax.dot_general(q, k, (((1,), (1,)), ((), ())), preferred_element_type=jnp.float32)
            top = jnp.max(scores, axis=1, keepdims=True)
            probs = jnp.exp2((scores - top) * coeff).astype(jnp.bfloat16)
            v = values[:, cut]
            v = jnp.concatenate([v, jnp.ones_like(v)], axis=1)
            out = jnp.dot(probs, v, preferred_element_type=jnp.float32)
            total = out[:, HEAD_DIM : HEAD_DIM + 1]
            out = (out[:, :HEAD_DIM] / total).astype(jnp.bfloat16)
            log = top * coeff + jnp.log(total) * math.log2(math.e)
            for g in range(group):
                part = slice(g * rows, (g + 1) * rows)
                so[j, :, (first + g) * HEAD_DIM : (first + g + 1) * HEAD_DIM] = out[part]
                logs = jnp.where(lane == first + g, log[part], logs)
        sl[j] = logs

        @pl.when(j > 0)
        def _():
            o_copy(j).start()
            l_copy(j).start()

        return carry

    lax.fori_loop(0, n, attend, 0)
    meta[...] = qall[:, :, features:]

    for j in range(1, n):
        l_copy(j).wait_recv()
        o_copy(j).wait_recv()
    logs = [sl[0]] + [rl[j] for j in range(1, n)]
    top = functools.reduce(jnp.maximum, logs)
    weights = [jnp.exp2(log - top) for log in logs]
    total = functools.reduce(jnp.add, weights)
    weights = [w / total for w in weights]
    for h in range(kv_local * group):
        cut = slice(h * HEAD_DIM, (h + 1) * HEAD_DIM)
        acc = weights[0][:, h : h + 1] * so[0, :, cut].astype(jnp.float32)
        for j in range(1, n):
            acc = acc + weights[j][:, h : h + 1] * ro[j, :, cut].astype(jnp.float32)
        attention_out[:, cut] = acc.astype(jnp.bfloat16)
        stream = (residual[:, cut].astype(jnp.float32) + acc).astype(jnp.bfloat16)
        column = pl.multiple_of(my_e * features + h * HEAD_DIM, HEAD_DIM)
        gathered[pl.ds(pl.multiple_of(me * rows, rows), rows), pl.ds(column, HEAD_DIM)] = stream

    def place(owner, k):
        column = (my_e + n_e - k) % n_e
        return gathered.at[
            pl.ds(pl.multiple_of(owner * rows, rows), rows),
            pl.ds(pl.multiple_of(column * features, features), features),
        ]

    def z_copy(k, slot):
        return remote(place(me, 0), slot, z_send.at[k], z_recv.at[k], "expert", (my_e + k) % n_e)

    def c_copy(j, k, slot):
        peer = ((chip + j) % half) * 2 + core
        return remote(place(me, k), slot, c_send.at[j, k], c_recv.at[j, k], "dp", peer)

    def s_copy(j, k, slot):
        owner = ((chip + half - j) % half) * 2 + core
        return remote(place(owner, k), slot, s_send.at[j, k], s_recv.at[j, k], "dp", sibling)

    for k in range(1, n_e):
        z_copy(k, place(me, 0)).start()
    for k in range(n_e):
        if k > 0:
            z_copy(k, place(me, k)).wait_recv()
        for j in range(1, half):
            c_copy(j, k, place(me, k)).start()
        s_copy(0, k, place(me, k)).start()
    for k in range(n_e):
        for j in range(1, half):
            owner = ((chip + half - j) % half) * 2 + core
            c_copy(j, k, place(owner, k)).wait_recv()
            s_copy(j, k, place(owner, k)).start()
    for k in range(n_e):
        for j in range(half):
            owner = ((chip + half - j) % half) * 2 + (1 - core)
            s_copy(j, k, place(owner, k)).wait_recv()
    for j in range(1, n):
        q_copy(j, me).wait_send()
        o_copy(j).wait_send()
        l_copy(j).wait_send()
    for k in range(n_e):
        if k > 0:
            z_copy(k, place(me, 0)).wait_send()
        for j in range(half):
            if j > 0:
                c_copy(j, k, place(me, k)).wait_send()
            s_copy(j, k, place(me, k)).wait_send()


def attend_and_gather(qx, keys, values, hot, residual, n, n_e):
    rows, features = residual.shape
    kv_local = keys.shape[1] // HEAD_DIM
    group = Q_HEADS // KV_HEADS
    half = n // 2
    bf16, f32 = jnp.bfloat16, jnp.float32
    dma = pltpu.SemaphoreType.DMA
    return pl.pallas_call(
        functools.partial(attention_kernel, n, n_e, kv_local, group),
        out_shape=(
            jax.ShapeDtypeStruct((rows, features), bf16),
            jax.ShapeDtypeStruct((n * rows, n_e * features), bf16),
            jax.ShapeDtypeStruct((n, rows, 128), bf16),
        ),
        in_specs=[whole()] * 5,
        out_specs=(whole(), whole(), whole()),
        scratch_shapes=[
            VMEM((n, rows, features + 128), bf16),
            VMEM((n, rows, features), bf16),
            VMEM((n, rows, 128), f32),
            VMEM((n, rows, features), bf16),
            VMEM((n, rows, 128), f32),
        ]
        + [dma((n,))] * 6
        + [dma((n_e,))] * 2
        + [dma((half, n_e))] * 4,
        compiler_params=pltpu.CompilerParams(
            collective_id=0, has_side_effects=True, vmem_limit_bytes=56 * 2**20
        ),
        name="attention_gather",
    )(qx, keys, values, hot, residual)


def expert_kernel(steps, chunk, stream, gain, target, weight, w_gate, w_up, w_down, out, rows_in, acc):
    x, f = pl.program_id(0), pl.program_id(1)
    tokens, width = stream.shape
    slots = acc.shape[0]
    per = slots // pl.num_programs(0)

    @pl.when((x == 0) & (f == 0))
    def _():
        spot = lax.broadcasted_iota(jnp.int32, (tokens, slots), 1)
        pick = (spot == target[:, 0:1]) | (spot == target[:, 1:2])
        pick = pick.astype(jnp.float32).astype(jnp.bfloat16)

        def norm(i, carry):
            cut = pl.ds(pl.multiple_of(i * 64, 64), 64)
            wide = stream[cut, :].astype(jnp.float32)
            inverse = lax.rsqrt(jnp.mean(wide * wide, axis=1, keepdims=True) + EPS)
            out[cut, :] = (wide * inverse * gain[...].astype(jnp.float32)).astype(jnp.bfloat16)
            return carry

        lax.fori_loop(0, tokens // 64, norm, 0)

        def choose(i, carry):
            cut = pl.ds(pl.multiple_of(i * chunk, chunk), chunk)
            rows_in[:, cut] = lax.dot_general(
                pick, out[:, cut], (((0,), (0,)), ((), ())), preferred_element_type=jnp.float32
            ).astype(jnp.bfloat16)
            return carry

        lax.fori_loop(0, width // chunk, choose, 0)

    mine = pl.ds(pl.multiple_of(x * per, per), per)
    data = rows_in[mine, :]
    gate = jnp.dot(data, w_gate[0], preferred_element_type=jnp.float32)
    up = jnp.dot(data, w_up[0], preferred_element_type=jnp.float32)
    hidden = (gate / (1.0 + jnp.exp(-gate)) * up).astype(jnp.bfloat16)

    def down(i, carry):
        cut = pl.ds(pl.multiple_of(i * chunk, chunk), chunk)
        term = jnp.dot(hidden, w_down[0, :, cut], preferred_element_type=jnp.float32)

        @pl.when(f == 0)
        def _():
            acc[mine, cut] = term

        @pl.when(f > 0)
        def _():
            acc[mine, cut] += term

        return carry

    lax.fori_loop(0, width // chunk, down, 0)

    @pl.when((x == pl.num_programs(0) - 1) & (f == steps - 1))
    def _():
        spot = lax.broadcasted_iota(jnp.int32, (tokens, slots), 1)
        mix = jnp.where(spot == target[:, 0:1], weight[:, 0:1], 0.0)
        mix = mix + jnp.where(spot == target[:, 1:2], weight[:, 1:2], 0.0)
        mix = mix.astype(jnp.bfloat16)

        def combine(i, carry):
            cut = pl.ds(pl.multiple_of(i * chunk, chunk), chunk)
            out[:, cut] = jnp.dot(
                mix, acc[:, cut].astype(jnp.bfloat16), preferred_element_type=jnp.float32
            ).astype(jnp.bfloat16)
            return carry

        lax.fori_loop(0, width // chunk, combine, 0)


def run_experts(stream, gain, target, weight, w_gate, w_up, w_down, slots):
    tokens, width = stream.shape
    local, _, hidden = w_gate.shape
    tile = 256 if hidden % 256 == 0 else 128
    steps = hidden // tile
    fixed = lambda x, f: (0, 0)
    once = pl.Buffered(1)
    return pl.pallas_call(
        functools.partial(expert_kernel, steps, 512),
        grid=(local, steps),
        out_shape=jax.ShapeDtypeStruct((tokens, width), jnp.bfloat16),
        in_specs=[
            pl.BlockSpec((tokens, width), fixed, pipeline_mode=once),
            pl.BlockSpec((1, width), fixed),
            pl.BlockSpec((tokens, 2), fixed),
            pl.BlockSpec((tokens, 2), fixed),
            pl.BlockSpec((1, width, tile), lambda x, f: (x, 0, f)),
            pl.BlockSpec((1, width, tile), lambda x, f: (x, 0, f)),
            pl.BlockSpec((1, tile, width), lambda x, f: (x, f, 0)),
        ],
        out_specs=pl.BlockSpec((tokens, width), fixed, pipeline_mode=once),
        scratch_shapes=[VMEM((slots, width), jnp.bfloat16), VMEM((slots, width), jnp.float32)],
        compiler_params=pltpu.CompilerParams(
            dimension_semantics=("arbitrary", "arbitrary"), vmem_limit_bytes=58 * 2**20
        ),
        name="experts",
    )(stream, gain, target, weight, w_gate, w_up, w_down)


def scatter_kernel(
    n, n_e, part, stream, out, buf_s, acc, buf_c, zsend, buf_z,
    s_send, s_recv, c_send, c_recv, z_send, z_recv,
):
    me, my_e = lax.axis_index("dp"), lax.axis_index("expert")
    rows, features = out.shape
    half = n // 2
    chip, core = me // 2, me % 2
    sibling = chip * 2 + (1 - core)
    greet(
        [((chip + j) % half) * 2 + core for j in range(1, half)] + [sibling],
        [(my_e + k) % n_e for k in range(1, n_e)],
    )

    def spot(j, k, side):
        owner = ((chip + j) % half) * 2 + side
        column = (my_e + k) % n_e
        return (
            pl.ds(pl.multiple_of(owner * rows, rows), rows),
            pl.ds(pl.multiple_of(column * features, features), features),
        )

    def s_copy(j, k):
        return remote(
            part.at[spot(j, k, 1 - core)], buf_s.at[j, k], s_send.at[j, k], s_recv.at[j, k], "dp", sibling
        )

    def c_copy(j, k):
        peer = ((chip + j) % half) * 2 + core
        return remote(acc.at[j, k], buf_c.at[j, k], c_send.at[j, k], c_recv.at[j, k], "dp", peer)

    def z_copy(k):
        return remote(zsend.at[k], buf_z.at[k], z_send.at[k], z_recv.at[k], "expert", (my_e + k) % n_e)

    far = [j for j in range(1, half)] + [0]
    columns = [k for k in range(1, n_e)] + [0]
    for k in columns:
        for j in far:
            s_copy(j, k).start()
    for k in columns:
        for j in far:
            s_copy(j, k).wait_recv()
            total = part[spot(j, k, core)].astype(jnp.float32) + buf_s[j, k].astype(jnp.float32)
            acc[j, k] = total.astype(jnp.bfloat16)
            if j > 0:
                c_copy(j, k).start()
    for k in columns:
        total = acc[0, k].astype(jnp.float32)
        for j in range(1, half):
            c_copy(j, k).wait_recv()
            total = total + buf_c[j, k].astype(jnp.float32)
        zsend[k] = total.astype(jnp.bfloat16)
        if k > 0:
            z_copy(k).start()
    total = zsend[0].astype(jnp.float32)
    for k in range(1, n_e):
        z_copy(k).wait_recv()
        total = total + buf_z[k].astype(jnp.float32)
    own = stream[spot(0, 0, core)].astype(jnp.float32)
    out[...] = (own + total).astype(jnp.bfloat16)
    for k in range(n_e):
        for j in range(half):
            s_copy(j, k).wait_send()
            if j > 0:
                c_copy(j, k).wait_send()
        if k > 0:
            z_copy(k).wait_send()


def sum_and_scatter(part, stream, n, n_e):
    rows, features = part.shape[0] // n, part.shape[1] // n_e
    half = n // 2
    bf16 = jnp.bfloat16
    dma = pltpu.SemaphoreType.DMA
    return pl.pallas_call(
        functools.partial(scatter_kernel, n, n_e),
        out_shape=jax.ShapeDtypeStruct((rows, features), bf16),
        in_specs=[whole()] * 2,
        out_specs=whole(),
        scratch_shapes=[
            VMEM((half, n_e, rows, features), bf16),
            VMEM((half, n_e, rows, features), bf16),
            VMEM((half, n_e, rows, features), bf16),
            VMEM((n_e, rows, features), bf16),
            VMEM((n_e, rows, features), bf16),
        ]
        + [dma((half, n_e))] * 4
        + [dma((n_e,))] * 2,
        compiler_params=pltpu.CompilerParams(
            collective_id=1, has_side_effects=True, vmem_limit_bytes=48 * 2**20
        ),
        name="sum_scatter",
    )(part, stream)


def body(
    residual, queries, cache_keys, cache_values, node_of_position, parent, leaf_ids, routes,
    gate_weights, norm_gain, w_gate, w_up, w_down,
):
    n, n_e = lax.axis_size("dp"), lax.axis_size("expert")
    rows = queries.shape[0]
    nodes = parent.shape[0]
    local = w_gate.shape[0]
    bf16 = jnp.bfloat16
    side = jnp.arange(128, dtype=jnp.int32)[None, :]
    node_range = jnp.arange(nodes, dtype=jnp.int32)[None, :]

    def parent_of(ids):
        return jnp.sum(jnp.where(ids[:, None] == node_range, parent[None, :], 0), axis=1)

    middle = parent_of(leaf_ids)
    upper = parent_of(middle)
    seen = (side == leaf_ids[:, None]) | (side == middle[:, None]) | (side == upper[:, None])

    flat = routes.reshape(-1)
    same = flat[:, None] == flat[None, :]
    order = jnp.arange(flat.shape[0], dtype=jnp.int32)
    ranks = jnp.sum((same & (order[None, :] < order[:, None])).astype(jnp.int32), axis=1).reshape(rows, 2)
    values = jnp.where(seen, 0.0, HIDE)
    info = jnp.concatenate(
        [routes.astype(jnp.float32), ranks.astype(jnp.float32), gate_weights.astype(jnp.float32)], axis=1
    )
    info = jnp.pad(info, ((0, 0), (META, 128 - META - 6)))
    values = jnp.where(side >= META, info, values).astype(bf16)
    qx = jnp.concatenate([queries, values], axis=1)
    column = jnp.where(node_of_position < 0, EMPTY, node_of_position)
    hot = (column[:, None] == side).astype(bf16)

    attention_out, stream, meta = attend_and_gather(qx, cache_keys, cache_values, hot, residual, n, n_e)

    info = meta[:, :, META : META + 6].astype(jnp.float32).reshape(n * rows, 6)
    expert = info[:, 0:2].astype(jnp.int32) - lax.axis_index("expert") * local
    owner = jnp.arange(n * rows, dtype=jnp.int32)[:, None] // rows
    target = expert * (n * CAP) + owner * CAP + info[:, 2:4].astype(jnp.int32)
    target = jnp.where((expert >= 0) & (expert < local), target, -1)
    part = run_experts(
        stream, norm_gain.reshape(1, -1), target, info[:, 4:6], w_gate, w_up, w_down, local * n * CAP
    )
    layer_out = sum_and_scatter(part, stream, n, n_e)
    return attention_out, layer_out


def solution(mesh):
    in_specs = (
        P("dp", "expert"),
        P("dp", "expert"),
        P("dp", "expert"),
        P("dp", "expert"),
        P("dp"),
        P(),
        P("dp"),
        P("dp", None),
        P("dp", None),
        P(),
        P("expert", None, "dp"),
        P("expert", None, "dp"),
        P("expert", "dp", None),
    )
    out_specs = (P("dp", "expert"), P("dp", "expert"))
    return jax.shard_map(body, mesh=mesh, in_specs=in_specs, out_specs=out_specs, check_vma=False)
```

time: 724 us -> 181 us (0.25)
  waiting for transfers between devices: 318 us -> 0 us
  Pallas kernels: 0 us -> 161 us
  matrix products: 123 us -> 0 us
  local copies, waits for them, and re-layouts: 96.7 us -> 8.59 us
  loops' own time: 84.8 us -> 0 us
  other arithmetic: 35.6 us -> 8.14 us
  blocking collectives: 24.9 us -> 0 us
  starting transfers between devices: 16.9 us -> 0 us
  between operations: 14.7 us -> 0.71 us
    reduce_scatter x1 -> x0, waiting for transfers between devices: 182 us -> none  [body(): lax.psum_scatter(lax.map(one_pair, pair_list).reshape(row_count * lax.axi...]
    pallas_call x0 -> x3, Pallas kernels: none -> 161 us  [the longest x1 67.1 us: run_experts(): pl.pallas_call(functools.partial(expert_kernel, steps, 512), grid=(local,...]
    dot_general x37 -> x0, matrix products: 123 us -> none  [the longest x32 36.3 us: one_pair(): jnp.dot(mixing, columns.reshape(capacity * local_experts, feature_count),...]
    all_to_all x4 -> x0, waiting for transfers between devices: 92.6 us -> none  [the longest x1 71.1 us: body(): lax.all_to_all(gathered, 'expert', split_axis=1, concat_axis=2, tiled=True)]
    another operation x1 -> x0, loops' own time: 84.8 us -> none  [body(): lax.map(one_pair, pair_list)]
    dynamic_slice x97 -> x0, local copies, waits for them, and re-layouts: 60.4 us -> none  [the longest x64 41.6 us: one_pair(): lax.dynamic_slice_in_dim(outs_block, feature_block * feature_count, featu...]
    all_gather x2 -> x0, waiting for transfers between devices: 43 us -> none  [the longest x1 36 us: body(): gathered = lax.all_gather(slot_data, 'dp', axis=0, tiled=True)]
    reduce_sum x10 -> x3, other arithmetic: 23.2 us -> 1.68 us  [the longest x2 1.5 us: parent_of(): jnp.sum(jnp.where(ids[:, None] == node_range, parent[None, :], 0), axis=1)]
  transfers between devices with their start and end apart: 7 -> 0, of which waited for: 6 -> 0; matrix products, arithmetic and copies ran while one was open for 6% -> 0% of each run, Pallas kernels for 0% -> 0%
where the time goes in v1:
time: 181 us; the launch traced here: 178 us
  Pallas kernels  161 us (89%)
  local copies, waits for them, and re-layouts  8.59 us (5%)
  other arithmetic  8.14 us (4%)
    pallas_call x1, Pallas kernels, run_experts(): pl.pallas_call(functools.partial(expert_kernel, steps, 512), grid=(local,...  67.1 us
    pallas_call x1, Pallas kernels, attend_and_gather(): pl.pallas_call(functools.partial(attention_kernel, n, n_e, kv_local, grou...  61.9 us
    pallas_call x1, Pallas kernels, sum_and_scatter(): pl.pallas_call(functools.partial(scatter_kernel, n, n_e), out_shape=jax.S...  31.8 us
    unnamed x7, local copies, waits for them, and re-layouts  4.27 us

profile of v1, /device:TPU:24, one launch (start us, length us, event | category | flops | bytes accessed | tf_op | source)
XLA Modules:
  0.0 178.3 jit_solution(10134012796670053377)
XLA Ops:
  0.6 0.8 select_reduce_fusion.1
  1.4 0.7 select_reduce_fusion
  2.1 0.7 convert_element_type.30
  2.8 0.7 compare_select_fusion
  3.5 0.1 copy.28
  3.7 0.8 copy.29
  4.4 1.3 reshape.66.gain
  5.7 0.8 copy.27
  6.5 0.1 eq.44
  6.6 0.2 convert_reduce_fusion
  6.8 0.2 convert_element_type.33
  7.0 0.8 fusion.6
  7.8 1.6 pad_maximum_fusion.qx
  9.3 1.8 fusion.hot
  11.1 61.9 %attention_gather.1 = (bf16[64,1024]{1,0:T(8,128)(2,1)}, bf16[512,4096]{1,0:T(8,128)(2,1)}, bf16[8,64,128]{2,1,0:T(8,128)(2,1)}) custom-call(bf16[64,1152]{1,0:T(8,128)(2,1)} %pad_maximum_fusion.qx, bf16[2304,256]{1,0:T(8,128)(2,1)} %keys.1, bf16[2304,256]{1,0:T(8,128)(2,1)} %values.1, bf16[2304,128]{1,0:T(8,128)(2,1)} %fusion.hot, bf16[64,1024]{1,0:T(8,128)(2,1)} %residual.1), custom_call_target="tpu_custom_call" | custom-call | tf_op jit(solution)/shard_map/attention_gather/pallas_call | solution.py:190
  73.1 1.0 slice.12
  74.1 0.9 fusion.2.target
  75.0 0.8 slice.18.weight
  75.9 67.1 %experts.1.part = bf16[512,4096]{1,0:T(8,128)(2,1)} custom-call(bf16[512,4096]{1,0:T(8,128)(2,1)} %get-tuple-element.6.stream, bf16[1,4096]{1,0:T(2,128)(2,1)} %reshape.66.gain, s32[512,2]{1,0:T(8,128)} %fusion.2.target, f32[512,2]{1,0:T(8,128)} %slice.18.weight, bf16[2,4096,1792]{2,1,0:T(8,128)(2,1)} %w_gate.1, bf16[2,4096,1792]{2,1,0:T(8,128)(2,1)} %w_up.1, ...), custom_call_target="tpu_custom_call" | custom-call | tf_op jit(solution)/shard_map/experts/pallas_call | solution.py:292
  143.0 0.0 copy-start
  143.0 2.2 %copy-done = bf16[512,4096]{1,0:T(8,128)(2,1)S(1)} copy-done((bf16[512,4096]{1,0:T(8,128)(2,1)S(1)}, bf16[512,4096]{1,0:T(8,128)(2,1)}, u32[]{:S(2)}) %copy-start) | copy-done | bytes 4194328
  145.2 0.0 copy-start.1
  145.2 31.8 %sum_scatter.1 = bf16[64,1024]{1,0:T(8,128)(2,1)S(1)} custom-call(bf16[512,4096]{1,0:T(8,128)(2,1)S(1)} %copy-done, bf16[512,4096]{1,0:T(8,128)(2,1)} %get-tuple-element.6.stream), custom_call_target="tpu_custom_call" | custom-call | tf_op jit(solution)/shard_map/sum_scatter/pallas_call | solution.py:388
  176.9 0.0 copy-done.1
  176.9 0.7 copy.32
  177.6 0.7 copy.33
  (4 shorter events, 0.0 us)
Async XLA Ops:
  143.0 2.2 %copy-start = (bf16[512,4096]{1,0:T(8,128)(2,1)S(1)}, bf16[512,4096]{1,0:T(8,128)(2,1)}, u32[]{:S(2)}) copy-start(bf16[512,4096]{1,0:T(8,128)(2,1)} %experts.1.part) | copy-start | bytes 12582916
  145.2 31.8 %copy-start.1 = (bf16[64,1024]{1,0:T(8,128)(2,1)S(1)}, bf16[64,1024]{1,0:T(8,128)(2,1)}, u32[]{:S(2)}) copy-start(bf16[64,1024]{1,0:T(8,128)(2,1)} %get-tuple-element.10) | copy-start | bytes 393220

commit v2 on v1

--- a/solution.py
+++ b/solution.py
@@ -31,7 +31,35 @@
         pl.semaphore_signal(barrier, inc=1, device_id={"dp": peer}, device_id_type=MESH)
     for peer in expert_peers:
         pl.semaphore_signal(barrier, inc=1, device_id={"expert": peer}, device_id_type=MESH)
-    pl.semaphore_wait(barrier, len(dp_peers) + len(expert_peers))
+    return lambda: pl.semaphore_wait(barrier, len(dp_peers) + len(expert_peers))
+
+
+def side_values(parent, leaf, routes, gate_weights):
+    rows = leaf.shape[1]
+
+    def parent_of(ids):
+        found = jnp.zeros_like(ids)
+        for node in range(parent.shape[0]):
+            found = jnp.where(ids == node, parent[node], found)
+        return found
+
+    own = leaf[...]
+    middle = parent_of(own)
+    upper = parent_of(middle)
+    place = lax.broadcasted_iota(jnp.int32, (128, rows), 0)
+    seen = (place == own) | (place == middle) | (place == upper)
+    named = [routes[0:1, :], routes[1:2, :]]
+    expert = lax.broadcasted_iota(jnp.int32, (EXPERTS, rows), 0)
+    hot = ((expert == named[0]) | (expert == named[1])).astype(jnp.float32)
+    before = lax.broadcasted_iota(jnp.int32, (rows, rows), 0) < lax.broadcasted_iota(jnp.int32, (rows, rows), 1)
+    count = jnp.dot(hot, before.astype(jnp.float32), preferred_element_type=jnp.float32)
+    ranks = [jnp.sum(jnp.where(expert == e, count, 0.0), axis=0, keepdims=True) for e in named]
+    weights = gate_weights[...].astype(jnp.float32)
+    info = [e.astype(jnp.float32) for e in named] + ranks + [weights[0:1, :], weights[1:2, :]]
+    values = jnp.where(place >= META, 0.0, jnp.where(seen, 0.0, HIDE))
+    for i, row in enumerate(info):
+        values = jnp.where(place == META + i, row, values)
+    return values.T.astype(jnp.bfloat16)
 
 
 def remote(src, dst, send, recv, axis, peer):
@@ -42,9 +70,9 @@
 
 def attention_kernel(
     n, n_e, kv_local, group,
-    qx, keys, values, hot, residual,
+    queries, parent, leaf, routes, gate_weights, node, keys, values, residual,
     attention_out, gathered, meta,
-    qall, so, sl, ro, rl,
+    hot, qall, so, sl, ro, rl,
     q_send, q_recv, o_send, o_recv, l_send, l_recv, z_send, z_recv, c_send, c_recv, s_send, s_recv,
 ):
     me, my_e = lax.axis_index("dp"), lax.axis_index("expert")
@@ -53,14 +81,18 @@
     chip, core = me // 2, me % 2
     sibling = chip * 2 + (1 - core)
     coeff = math.log2(math.e) / math.sqrt(HEAD_DIM)
-    greet([(me + j) % n for j in range(1, n)], [(my_e + k) % n_e for k in range(1, n_e)])
+    wait_all = greet([(me + j) % n for j in range(1, n)], [(my_e + k) % n_e for k in range(1, n_e)])
+    qall[me] = jnp.concatenate([queries[...], side_values(parent, leaf, routes, gate_weights)], axis=1)
+    wait_all()
 
     def q_copy(j, slot):
-        return remote(qx, qall.at[slot], q_send.at[j], q_recv.at[j], "dp", (me + j) % n)
+        return remote(qall.at[me], qall.at[slot], q_send.at[j], q_recv.at[j], "dp", (me + j) % n)
 
     for j in range(1, n):
         q_copy(j, me).start()
-    qall[me] = qx[...]
+    node_row = jnp.where(node[...] < 0, EMPTY, node[...])
+    spread = lax.broadcasted_iota(jnp.int32, (128, node.shape[1]), 0) == node_row
+    hot[...] = spread.astype(jnp.float32).T.astype(jnp.bfloat16)
 
     def o_copy(j):
         return remote(so.at[j], ro.at[j], o_send.at[j], o_recv.at[j], "dp", (me + n - j) % n)
@@ -180,7 +212,7 @@
             s_copy(j, k, place(me, k)).wait_send()
 
 
-def attend_and_gather(qx, keys, values, hot, residual, n, n_e):
+def attend_and_gather(queries, parent, leaf, routes, gate_weights, node, keys, values, residual, n, n_e):
     rows, features = residual.shape
     kv_local = keys.shape[1] // HEAD_DIM
     group = Q_HEADS // KV_HEADS
@@ -194,9 +226,10 @@
             jax.ShapeDtypeStruct((n * rows, n_e * features), bf16),
             jax.ShapeDtypeStruct((n, rows, 128), bf16),
         ),
-        in_specs=[whole()] * 5,
+        in_specs=[whole(), whole(pltpu.SMEM)] + [whole()] * 7,
         out_specs=(whole(), whole(), whole()),
         scratch_shapes=[
+            VMEM((keys.shape[0], 128), bf16),
             VMEM((n, rows, features + 128), bf16),
             VMEM((n, rows, features), bf16),
             VMEM((n, rows, 128), f32),
@@ -210,105 +243,127 @@
             collective_id=0, has_side_effects=True, vmem_limit_bytes=56 * 2**20
         ),
         name="attention_gather",
-    )(qx, keys, values, hot, residual)
-
-
-def expert_kernel(steps, chunk, stream, gain, target, weight, w_gate, w_up, w_down, out, rows_in, acc):
+    )(queries, parent, leaf, routes, gate_weights, node, keys, values, residual)
+
+
+def expert_kernel(
+    k_steps, rows, stream, gain, meta, w_gate, w_up, w_down, out,
+    inverse, pick, mix, gate, up, hidden, outs,
+):
     x, f = pl.program_id(0), pl.program_id(1)
     tokens, width = stream.shape
-    slots = acc.shape[0]
-    per = slots // pl.num_programs(0)
+    local, per, _ = outs.shape
+    tile = w_gate.shape[1]
+    columns = w_down.shape[2]
+    base = lax.axis_index("expert") * local
+
+    def slot_keys(values, owner):
+        return [
+            (values[i].astype(jnp.int32) - base, owner * CAP + values[2 + i].astype(jnp.int32)) for i in range(2)
+        ]
 
     @pl.when((x == 0) & (f == 0))
     def _():
-        spot = lax.broadcasted_iota(jnp.int32, (tokens, slots), 1)
-        pick = (spot == target[:, 0:1]) | (spot == target[:, 1:2])
-        pick = pick.astype(jnp.float32).astype(jnp.bfloat16)
-
-        def norm(i, carry):
+        def square(i, carry):
             cut = pl.ds(pl.multiple_of(i * 64, 64), 64)
             wide = stream[cut, :].astype(jnp.float32)
-            inverse = lax.rsqrt(jnp.mean(wide * wide, axis=1, keepdims=True) + EPS)
-            out[cut, :] = (wide * inverse * gain[...].astype(jnp.float32)).astype(jnp.bfloat16)
+            mean = jnp.mean(wide * wide, axis=1, keepdims=True)
+            inverse[cut, :] = jnp.broadcast_to(lax.rsqrt(mean + EPS), (64, 128))
             return carry
 
-        lax.fori_loop(0, tokens // 64, norm, 0)
-
-        def choose(i, carry):
-            cut = pl.ds(pl.multiple_of(i * chunk, chunk), chunk)
-            rows_in[:, cut] = lax.dot_general(
-                pick, out[:, cut], (((0,), (0,)), ((), ())), preferred_element_type=jnp.float32
-            ).astype(jnp.bfloat16)
-            return carry
-
-        lax.fori_loop(0, width // chunk, choose, 0)
-
-    mine = pl.ds(pl.multiple_of(x * per, per), per)
-    data = rows_in[mine, :]
-    gate = jnp.dot(data, w_gate[0], preferred_element_type=jnp.float32)
-    up = jnp.dot(data, w_up[0], preferred_element_type=jnp.float32)
-    hidden = (gate / (1.0 + jnp.exp(-gate)) * up).astype(jnp.bfloat16)
-
-    def down(i, carry):
-        cut = pl.ds(pl.multiple_of(i * chunk, chunk), chunk)
-        term = jnp.dot(hidden, w_down[0, :, cut], preferred_element_type=jnp.float32)
+        lax.fori_loop(0, tokens // 64, square, 0)
+        info = meta[...].astype(jnp.float32)
+        values = [info[:, META + i : META + i + 1] for i in range(6)]
+        owner = lax.broadcasted_iota(jnp.int32, (tokens, 1), 0) // rows
+        spot = lax.broadcasted_iota(jnp.int32, (tokens, local * per), 1)
+        total = jnp.zeros((tokens, local * per), jnp.float32)
+        for i, (expert, slot) in enumerate(slot_keys(values, owner)):
+            target = jnp.where((expert >= 0) & (expert < local), expert * per + slot, -1)
+            total = total + jnp.where(spot == target, values[4 + i], 0.0)
+        mix[...] = total.astype(jnp.bfloat16)
+
+    @pl.when(f == 0)
+    def _():
+        info = meta[...].astype(jnp.float32).T
+        values = [info[META + i : META + i + 1, :] for i in range(4)]
+        owner = lax.broadcasted_iota(jnp.int32, (1, tokens), 1) // rows
+        spot = lax.broadcasted_iota(jnp.int32, (per, tokens), 0)
+        hits = [spot == jnp.where(expert == x, slot, -1) for expert, slot in slot_keys(values, owner)]
+        pick[...] = (hits[0] | hits[1]).astype(jnp.float32).astype(jnp.bfloat16)
+
+    @pl.when(f < k_steps)
+    def _():
+        cut = pl.ds(pl.multiple_of(f * tile, tile), tile)
+        wide = stream[:, cut].astype(jnp.float32)
+        normed = (wide * inverse[:, 0:1] * gain[:, cut].astype(jnp.float32)).astype(jnp.bfloat16)
+        data = jnp.dot(pick[...], normed, preferred_element_type=jnp.float32).astype(jnp.bfloat16)
+        gate_term = jnp.dot(data, w_gate[0], preferred_element_type=jnp.float32)
+        up_term = jnp.dot(data, w_up[0], preferred_element_type=jnp.float32)
 
         @pl.when(f == 0)
         def _():
-            acc[mine, cut] = term
+            gate[...] = gate_term
+            up[...] = up_term
 
         @pl.when(f > 0)
         def _():
-            acc[mine, cut] += term
-
-        return carry
-
-    lax.fori_loop(0, width // chunk, down, 0)
-
-    @pl.when((x == pl.num_programs(0) - 1) & (f == steps - 1))
+            gate[...] += gate_term
+            up[...] += up_term
+
+    @pl.when(f == k_steps - 1)
     def _():
-        spot = lax.broadcasted_iota(jnp.int32, (tokens, slots), 1)
-        mix = jnp.where(spot == target[:, 0:1], weight[:, 0:1], 0.0)
-        mix = mix + jnp.where(spot == target[:, 1:2], weight[:, 1:2], 0.0)
-        mix = mix.astype(jnp.bfloat16)
-
-        def combine(i, carry):
-            cut = pl.ds(pl.multiple_of(i * chunk, chunk), chunk)
-            out[:, cut] = jnp.dot(
-                mix, acc[:, cut].astype(jnp.bfloat16), preferred_element_type=jnp.float32
-            ).astype(jnp.bfloat16)
-            return carry
-
-        lax.fori_loop(0, width // chunk, combine, 0)
-
-
-def run_experts(stream, gain, target, weight, w_gate, w_up, w_down, slots):
+        value = gate[...]
+        hidden[...] = (value / (1.0 + jnp.exp(-value)) * up[...]).astype(jnp.bfloat16)
+
+    @pl.when(f >= k_steps)
+    def _():
+        cut = pl.ds(pl.multiple_of((f - k_steps) * columns, columns), columns)
+        term = jnp.dot(hidden[...], w_down[0], preferred_element_type=jnp.float32).astype(jnp.bfloat16)
+        outs[x, :, cut] = term
+
+        @pl.when(x == local - 1)
+        def _():
+            both = outs[:, :, cut].reshape(local * per, columns)
+            out[:, cut] = jnp.dot(mix[...], both, preferred_element_type=jnp.float32).astype(jnp.bfloat16)
+
+
+def run_experts(stream, gain, meta, w_gate, w_up, w_down, rows):
     tokens, width = stream.shape
     local, _, hidden = w_gate.shape
-    tile = 256 if hidden % 256 == 0 else 128
-    steps = hidden // tile
+    per = tokens // rows * CAP
+    tile = 512
+    k_steps = d_steps = width // tile
+    bf16, f32 = jnp.bfloat16, jnp.float32
     fixed = lambda x, f: (0, 0)
+    wide = lambda x, f: (x, jnp.minimum(f, k_steps - 1), 0)
     once = pl.Buffered(1)
     return pl.pallas_call(
-        functools.partial(expert_kernel, steps, 512),
-        grid=(local, steps),
-        out_shape=jax.ShapeDtypeStruct((tokens, width), jnp.bfloat16),
+        functools.partial(expert_kernel, k_steps, rows),
+        grid=(local, k_steps + d_steps),
+        out_shape=jax.ShapeDtypeStruct((tokens, width), bf16),
         in_specs=[
             pl.BlockSpec((tokens, width), fixed, pipeline_mode=once),
             pl.BlockSpec((1, width), fixed),
-            pl.BlockSpec((tokens, 2), fixed),
-            pl.BlockSpec((tokens, 2), fixed),
-            pl.BlockSpec((1, width, tile), lambda x, f: (x, 0, f)),
-            pl.BlockSpec((1, width, tile), lambda x, f: (x, 0, f)),
-            pl.BlockSpec((1, tile, width), lambda x, f: (x, f, 0)),
+            pl.BlockSpec((tokens, 128), fixed),
+            pl.BlockSpec((1, tile, hidden), wide),
+            pl.BlockSpec((1, tile, hidden), wide),
+            pl.BlockSpec((1, hidden, tile), lambda x, f: (x, 0, jnp.maximum(f - k_steps, 0))),
         ],
         out_specs=pl.BlockSpec((tokens, width), fixed, pipeline_mode=once),
-        scratch_shapes=[VMEM((slots, width), jnp.bfloat16), VMEM((slots, width), jnp.float32)],
+        scratch_shapes=[
+            VMEM((tokens, 128), f32),
+            VMEM((per, tokens), bf16),
+            VMEM((tokens, local * per), bf16),
+            VMEM((per, hidden), f32),
+            VMEM((per, hidden), f32),
+            VMEM((per, hidden), bf16),
+            VMEM((local, per, width), bf16),
+        ],
         compiler_params=pltpu.CompilerParams(
             dimension_semantics=("arbitrary", "arbitrary"), vmem_limit_bytes=58 * 2**20
         ),
         name="experts",
-    )(stream, gain, target, weight, w_gate, w_up, w_down)
+    )(stream, gain, meta, w_gate, w_up, w_down)
 
 
 def scatter_kernel(
@@ -320,10 +375,11 @@
     half = n // 2
     chip, core = me // 2, me % 2
     sibling = chip * 2 + (1 - core)
-    greet(
+    wait_all = greet(
         [((chip + j) % half) * 2 + core for j in range(1, half)] + [sibling],
         [(my_e + k) % n_e for k in range(1, n_e)],
     )
+    wait_all()
 
     def spot(j, k, side):
         owner = ((chip + j) % half) * 2 + side
@@ -412,42 +468,12 @@
 ):
     n, n_e = lax.axis_size("dp"), lax.axis_size("expert")
     rows = queries.shape[0]
-    nodes = parent.shape[0]
-    local = w_gate.shape[0]
-    bf16 = jnp.bfloat16
-    side = jnp.arange(128, dtype=jnp.int32)[None, :]
-    node_range = jnp.arange(nodes, dtype=jnp.int32)[None, :]
-
-    def parent_of(ids):
-        return jnp.sum(jnp.where(ids[:, None] == node_range, parent[None, :], 0), axis=1)
-
-    middle = parent_of(leaf_ids)
-    upper = parent_of(middle)
-    seen = (side == leaf_ids[:, None]) | (side == middle[:, None]) | (side == upper[:, None])
-
-    flat = routes.reshape(-1)
-    same = flat[:, None] == flat[None, :]
-    order = jnp.arange(flat.shape[0], dtype=jnp.int32)
-    ranks = jnp.sum((same & (order[None, :] < order[:, None])).astype(jnp.int32), axis=1).reshape(rows, 2)
-    values = jnp.where(seen, 0.0, HIDE)
-    info = jnp.concatenate(
-        [routes.astype(jnp.float32), ranks.astype(jnp.float32), gate_weights.astype(jnp.float32)], axis=1
+    attention_out, stream, meta = attend_and_gather(
+        queries, parent, leaf_ids.reshape(1, -1), routes.T, gate_weights.T, node_of_position.reshape(1, -1),
+        cache_keys, cache_values, residual, n, n_e,
     )
-    info = jnp.pad(info, ((0, 0), (META, 128 - META - 6)))
-    values = jnp.where(side >= META, info, values).astype(bf16)
-    qx = jnp.concatenate([queries, values], axis=1)
-    column = jnp.where(node_of_position < 0, EMPTY, node_of_position)
-    hot = (column[:, None] == side).astype(bf16)
-
-    attention_out, stream, meta = attend_and_gather(qx, cache_keys, cache_values, hot, residual, n, n_e)
-
-    info = meta[:, :, META : META + 6].astype(jnp.float32).reshape(n * rows, 6)
-    expert = info[:, 0:2].astype(jnp.int32) - lax.axis_index("expert") * local
-    owner = jnp.arange(n * rows, dtype=jnp.int32)[:, None] // rows
-    target = expert * (n * CAP) + owner * CAP + info[:, 2:4].astype(jnp.int32)
-    target = jnp.where((expert >= 0) & (expert < local), target, -1)
     part = run_experts(
-        stream, norm_gain.reshape(1, -1), target, info[:, 4:6], w_gate, w_up, w_down, local * n * CAP
+        stream, norm_gain.reshape(1, -1), meta.reshape(n * rows, 128), w_gate, w_up, w_down, rows
     )
     layer_out = sum_and_scatter(part, stream, n, n_e)
     return attention_out, layer_out

time: 181 us -> 166 us (0.917)
  other arithmetic: 8.14 us -> 0 us
  Pallas kernels: 161 us -> 156 us
  local copies, waits for them, and re-layouts: 8.59 us -> 6.13 us
    pallas_call x1, Pallas kernels: 67.1 us -> 61.9 us  [run_experts(): pl.pallas_call(functools.partial(expert_kernel, k_steps, rows), grid=(loc...]
    convert_element_type x4 -> x0, other arithmetic: 3.22 us -> none  [the longest x1 1.77 us: body(): hot = (column[:, None] == side).astype(bf16)]
    slice x2 -> x0, local copies, waits for them, and re-layouts: 1.85 us -> none  [the longest x1 1.01 us: body(): info = meta[:, :, META:META + 6].astype(jnp.float32).reshape(n * rows, 6)]
    unnamed x7 -> x6, local copies, waits for them, and re-layouts: 4.27 us -> 3.5 us
where the time goes in v2:
time: 166 us; the launch traced here: 162 us
  Pallas kernels  156 us (94%)
  local copies, waits for them, and re-layouts  6.13 us (4%)
    pallas_call x1, Pallas kernels, run_experts(): pl.pallas_call(functools.partial(expert_kernel, k_steps, rows), grid=(loc...  61.9 us
    pallas_call x1, Pallas kernels, attend_and_gather(): pl.pallas_call(functools.partial(attention_kernel, n, n_e, kv_local, grou...  61.8 us
    pallas_call x1, Pallas kernels, sum_and_scatter(): pl.pallas_call(functools.partial(scatter_kernel, n, n_e), out_shape=jax.S...  31.9 us
    unnamed x6, local copies, waits for them, and re-layouts  3.5 us

profile of v2, /device:TPU:24, one launch (start us, length us, event | category | flops | bytes accessed | tf_op | source)
XLA Modules:
  0.0 162.4 jit_solution(14086090440999292146)
XLA Ops:
  0.6 1.3 reshape.17.node
  1.9 1.3 reshape.18.gain
  3.3 61.8 %attention_gather.1 = (bf16[64,1024]{1,0:T(8,128)(2,1)}, bf16[512,4096]{1,0:T(8,128)(2,1)}, bf16[8,64,128]{2,1,0:T(8,128)(2,1)}) custom-call(bf16[64,1024]{1,0:T(8,128)(2,1)} %queries.1, s32[21]{0:T(128)} %parent.1, s32[1,64]{1,0:T(1,128)} %bitcast.6, s32[2,64]{1,0:T(2,128)} %bitcast.5, bf16[2,64]{1,0:T(2,128)(2,1)} %bitcast.7, s32[1,2304]{1,0:T(1,128)} %reshape.17.node, ...), custom_call_target="tpu_custom_call" | custom-call | tf_op jit(solution)/shard_map/attention_gather/pallas_call | solution.py:222
  65.1 61.9 %experts.1.part = bf16[512,4096]{1,0:T(8,128)(2,1)} custom-call(bf16[512,4096]{1,0:T(8,128)(2,1)} %get-tuple-element.6.stream, bf16[1,4096]{1,0:T(2,128)(2,1)} %reshape.18.gain, bf16[512,128]{1,0:T(8,128)(2,1)} %bitcast.4, bf16[2,4096,1792]{2,1,0:T(8,128)(2,1)} %w_gate.1, bf16[2,4096,1792]{2,1,0:T(8,128)(2,1)} %w_up.1, bf16[2,1792,4096]{2,1,0:T(8,128)(2,1)} %w_down.1), custom_call_target="tpu_custom_call" | custom-call | tf_op jit(solution)/shard_map/experts/pallas_call | solution.py:340
  127.0 0.0 copy-start
  127.0 2.2 %copy-done = bf16[512,4096]{1,0:T(8,128)(2,1)S(1)} copy-done((bf16[512,4096]{1,0:T(8,128)(2,1)S(1)}, bf16[512,4096]{1,0:T(8,128)(2,1)}, u32[]{:S(2)}) %copy-start) | copy-done | bytes 4194328
  129.2 0.0 copy-start.1
  129.2 31.9 %sum_scatter.1 = bf16[64,1024]{1,0:T(8,128)(2,1)S(1)} custom-call(bf16[512,4096]{1,0:T(8,128)(2,1)S(1)} %copy-done, bf16[512,4096]{1,0:T(8,128)(2,1)} %get-tuple-element.6.stream), custom_call_target="tpu_custom_call" | custom-call | tf_op jit(solution)/shard_map/sum_scatter/pallas_call | solution.py:444
  161.1 0.0 copy-done.1
  161.1 0.7 copy.17
  161.8 0.7 copy.18
Async XLA Ops:
  127.0 2.2 %copy-start = (bf16[512,4096]{1,0:T(8,128)(2,1)S(1)}, bf16[512,4096]{1,0:T(8,128)(2,1)}, u32[]{:S(2)}) copy-start(bf16[512,4096]{1,0:T(8,128)(2,1)} %experts.1.part) | copy-start | bytes 12582916
  129.2 31.9 %copy-start.1 = (bf16[64,1024]{1,0:T(8,128)(2,1)S(1)}, bf16[64,1024]{1,0:T(8,128)(2,1)}, u32[]{:S(2)}) copy-start(bf16[64,1024]{1,0:T(8,128)(2,1)} %get-tuple-element.10) | copy-start | bytes 393220

commit v3 on v2

--- a/solution.py
+++ b/solution.py
@@ -247,23 +247,37 @@
 
 
 def expert_kernel(
-    k_steps, rows, stream, gain, meta, w_gate, w_up, w_down, out,
-    inverse, pick, mix, gate, up, hidden, outs,
+    n, n_e, k_steps, stream, gain, meta, w_gate, w_up, w_down, out,
+    inverse, pick, mix, gate, up, hidden, outs, part, buf_s, acc, buf_c, zsend, buf_z, own,
+    s_send, s_recv, c_send, c_recv, z_send, z_recv,
 ):
-    x, f = pl.program_id(0), pl.program_id(1)
+    f = pl.program_id(0)
+    me, my_e = lax.axis_index("dp"), lax.axis_index("expert")
+    rows, features = out.shape
+    half = n // 2
+    chip, core = me // 2, me % 2
+    sibling = chip * 2 + (1 - core)
     tokens, width = stream.shape
-    local, per, _ = outs.shape
+    local, per, columns = outs.shape
     tile = w_gate.shape[1]
-    columns = w_down.shape[2]
-    base = lax.axis_index("expert") * local
+    base = my_e * local
+    first_down = local * k_steps
+    per_e = features // columns * local
+    last = n_e * per_e - 1
+    phase = f % k_steps
 
     def slot_keys(values, owner):
         return [
             (values[i].astype(jnp.int32) - base, owner * CAP + values[2 + i].astype(jnp.int32)) for i in range(2)
         ]
 
-    @pl.when((x == 0) & (f == 0))
+    @pl.when(f == 0)
     def _():
+        wait_all = greet(
+            [((chip + j) % half) * 2 + core for j in range(1, half)] + [sibling],
+            [(my_e + k) % n_e for k in range(1, n_e)],
+        )
+
         def square(i, carry):
             cut = pl.ds(pl.multiple_of(i * 64, 64), 64)
             wide = stream[cut, :].astype(jnp.float32)
@@ -281,185 +295,195 @@
             target = jnp.where((expert >= 0) & (expert < local), expert * per + slot, -1)
             total = total + jnp.where(spot == target, values[4 + i], 0.0)
         mix[...] = total.astype(jnp.bfloat16)
-
-    @pl.when(f == 0)
+        wait_all()
+
+    @pl.when((f < first_down) & (phase == 0))
     def _():
         info = meta[...].astype(jnp.float32).T
         values = [info[META + i : META + i + 1, :] for i in range(4)]
         owner = lax.broadcasted_iota(jnp.int32, (1, tokens), 1) // rows
         spot = lax.broadcasted_iota(jnp.int32, (per, tokens), 0)
+        x = f // k_steps
         hits = [spot == jnp.where(expert == x, slot, -1) for expert, slot in slot_keys(values, owner)]
         pick[...] = (hits[0] | hits[1]).astype(jnp.float32).astype(jnp.bfloat16)
 
-    @pl.when(f < k_steps)
+    @pl.when(f < first_down)
     def _():
-        cut = pl.ds(pl.multiple_of(f * tile, tile), tile)
+        cut = pl.ds(pl.multiple_of(phase * tile, tile), tile)
         wide = stream[:, cut].astype(jnp.float32)
         normed = (wide * inverse[:, 0:1] * gain[:, cut].astype(jnp.float32)).astype(jnp.bfloat16)
         data = jnp.dot(pick[...], normed, preferred_element_type=jnp.float32).astype(jnp.bfloat16)
         gate_term = jnp.dot(data, w_gate[0], preferred_element_type=jnp.float32)
         up_term = jnp.dot(data, w_up[0], preferred_element_type=jnp.float32)
 
-        @pl.when(f == 0)
+        @pl.when(phase == 0)
         def _():
             gate[...] = gate_term
             up[...] = up_term
 
-        @pl.when(f > 0)
+        @pl.when(phase > 0)
         def _():
             gate[...] += gate_term
             up[...] += up_term
 
-    @pl.when(f == k_steps - 1)
+    for x in range(local):
+        @pl.when(f == (x + 1) * k_steps - 1)
+        def _():
+            value = gate[...]
+            hidden[x] = (value / (1.0 + jnp.exp(-value)) * up[...]).astype(jnp.bfloat16)
+
+    @pl.when(f >= first_down)
     def _():
-        value = gate[...]
-        hidden[...] = (value / (1.0 + jnp.exp(-value)) * up[...]).astype(jnp.bfloat16)
-
-    @pl.when(f >= k_steps)
+        step = f - first_down
+        x = step % local
+        outs[x] = jnp.dot(hidden[x], w_down[0], preferred_element_type=jnp.float32).astype(jnp.bfloat16)
+
+        @pl.when(x == local - 1)
+        def _():
+            cut = pl.ds(pl.multiple_of(step // local * columns, columns), columns)
+            both = outs[...].reshape(local * per, columns)
+            part[:, cut] = jnp.dot(mix[...], both, preferred_element_type=jnp.float32).astype(jnp.bfloat16)
+
+    def spot(j, e, side):
+        owner = ((chip + j) % half) * 2 + side
+        return (pl.ds(pl.multiple_of(owner * rows, rows), rows), pl.ds(e * features, features))
+
+    def s_copy(j, e):
+        return remote(
+            part.at[spot(j, e, 1 - core)], buf_s.at[j, e], s_send.at[j, e], s_recv.at[j, e], "dp", sibling
+        )
+
+    def c_copy(j, e):
+        peer = ((chip + j) % half) * 2 + core
+        return remote(acc.at[j, e], buf_c.at[j, e], c_send.at[j, e], c_recv.at[j, e], "dp", peer)
+
+    def z_copy(e):
+        return remote(zsend.at[e], buf_z.at[my_e], z_send.at[e], z_recv.at[my_e], "expert", e)
+
+    def z_from(e):
+        return remote(zsend.at[e], buf_z.at[e], z_send.at[e], z_recv.at[e], "expert", e)
+
+    far = [j for j in range(1, half)] + [0]
+
+    def to_core(e):
+        for j in far:
+            s_copy(j, e).start()
+
+    def to_chips(e):
+        for j in far:
+            s_copy(j, e).wait_recv()
+            total = part[spot(j, e, core)].astype(jnp.float32) + buf_s[j, e].astype(jnp.float32)
+            acc[j, e] = total.astype(jnp.bfloat16)
+            if j > 0:
+                c_copy(j, e).start()
+
+    def to_expert(e):
+        total = acc[0, e].astype(jnp.float32)
+        for j in range(1, half):
+            c_copy(j, e).wait_recv()
+            total = total + buf_c[j, e].astype(jnp.float32)
+
+        @pl.when(my_e == e)
+        def _():
+            own[...] = total
+
+        @pl.when(my_e != e)
+        def _():
+            zsend[e] = total.astype(jnp.bfloat16)
+            z_copy(e).start()
+
+    events = []
+    for e in range(n_e):
+        events.append(((e + 1) * per_e - 1, 0, to_core, e))
+        events.append(((e + 1) * per_e, 1, to_chips, e))
+        events.append(((e + 2) * per_e, 2, to_expert, e))
+    events.sort(key=lambda event: (event[0], event[1], event[3]))
+    for at, _, act, e in events:
+        pl.when(f == first_down + min(at, last))(functools.partial(act, e))
+
+    @pl.when(f == first_down + last)
     def _():
-        cut = pl.ds(pl.multiple_of((f - k_steps) * columns, columns), columns)
-        term = jnp.dot(hidden[...], w_down[0], preferred_element_type=jnp.float32).astype(jnp.bfloat16)
-        outs[x, :, cut] = term
-
-        @pl.when(x == local - 1)
-        def _():
-            both = outs[:, :, cut].reshape(local * per, columns)
-            out[:, cut] = jnp.dot(mix[...], both, preferred_element_type=jnp.float32).astype(jnp.bfloat16)
-
-
-def run_experts(stream, gain, meta, w_gate, w_up, w_down, rows):
+        for e in range(n_e):
+            @pl.when(my_e != e)
+            def _():
+                z_from(e).wait_recv()
+                own[...] += buf_z[e].astype(jnp.float32)
+
+        mine = (
+            pl.ds(pl.multiple_of(me * rows, rows), rows),
+            pl.ds(pl.multiple_of(my_e * features, features), features),
+        )
+        out[...] = (stream[mine].astype(jnp.float32) + own[...]).astype(jnp.bfloat16)
+        for e in range(n_e):
+            for j in range(half):
+                s_copy(j, e).wait_send()
+                if j > 0:
+                    c_copy(j, e).wait_send()
+
+            @pl.when(my_e != e)
+            def _():
+                z_copy(e).wait_send()
+
+
+def run_experts(stream, gain, meta, w_gate, w_up, w_down, n, n_e):
     tokens, width = stream.shape
+    rows, features = tokens // n, width // n_e
+    half = n // 2
     local, _, hidden = w_gate.shape
-    per = tokens // rows * CAP
+    per = n * CAP
     tile = 512
-    k_steps = d_steps = width // tile
+    k_steps = width // tile
+    first_down = local * k_steps
     bf16, f32 = jnp.bfloat16, jnp.float32
-    fixed = lambda x, f: (0, 0)
-    wide = lambda x, f: (x, jnp.minimum(f, k_steps - 1), 0)
+    dma = pltpu.SemaphoreType.DMA
+    fixed = lambda f: (0, 0)
+
+    def wide(f):
+        step = jnp.minimum(f, first_down - 1)
+        return (step // k_steps, step % k_steps, 0)
+
+    def tall(f):
+        step = jnp.maximum(f - first_down, 0)
+        return (step % local, 0, step // local)
+
     once = pl.Buffered(1)
     return pl.pallas_call(
-        functools.partial(expert_kernel, k_steps, rows),
-        grid=(local, k_steps + d_steps),
-        out_shape=jax.ShapeDtypeStruct((tokens, width), bf16),
+        functools.partial(expert_kernel, n, n_e, k_steps),
+        grid=(2 * first_down,),
+        out_shape=jax.ShapeDtypeStruct((rows, features), bf16),
         in_specs=[
             pl.BlockSpec((tokens, width), fixed, pipeline_mode=once),
             pl.BlockSpec((1, width), fixed),
             pl.BlockSpec((tokens, 128), fixed),
             pl.BlockSpec((1, tile, hidden), wide),
             pl.BlockSpec((1, tile, hidden), wide),
-            pl.BlockSpec((1, hidden, tile), lambda x, f: (x, 0, jnp.maximum(f - k_steps, 0))),
+            pl.BlockSpec((1, hidden, tile), tall),
         ],
-        out_specs=pl.BlockSpec((tokens, width), fixed, pipeline_mode=once),
+        out_specs=pl.BlockSpec((rows, features), fixed),
         scratch_shapes=[
             VMEM((tokens, 128), f32),
             VMEM((per, tokens), bf16),
             VMEM((tokens, local * per), bf16),
             VMEM((per, hidden), f32),
             VMEM((per, hidden), f32),
-            VMEM((per, hidden), bf16),
-            VMEM((local, per, width), bf16),
-        ],
-        compiler_params=pltpu.CompilerParams(
-            dimension_semantics=("arbitrary", "arbitrary"), vmem_limit_bytes=58 * 2**20
-        ),
-        name="experts",
-    )(stream, gain, meta, w_gate, w_up, w_down)
-
-
-def scatter_kernel(
-    n, n_e, part, stream, out, buf_s, acc, buf_c, zsend, buf_z,
-    s_send, s_recv, c_send, c_recv, z_send, z_recv,
-):
-    me, my_e = lax.axis_index("dp"), lax.axis_index("expert")
-    rows, features = out.shape
-    half = n // 2
-    chip, core = me // 2, me % 2
-    sibling = chip * 2 + (1 - core)
-    wait_all = greet(
-        [((chip + j) % half) * 2 + core for j in range(1, half)] + [sibling],
-        [(my_e + k) % n_e for k in range(1, n_e)],
-    )
-    wait_all()
-
-    def spot(j, k, side):
-        owner = ((chip + j) % half) * 2 + side
-        column = (my_e + k) % n_e
-        return (
-            pl.ds(pl.multiple_of(owner * rows, rows), rows),
-            pl.ds(pl.multiple_of(column * features, features), features),
-        )
-
-    def s_copy(j, k):
-        return remote(
-            part.at[spot(j, k, 1 - core)], buf_s.at[j, k], s_send.at[j, k], s_recv.at[j, k], "dp", sibling
-        )
-
-    def c_copy(j, k):
-        peer = ((chip + j) % half) * 2 + core
-        return remote(acc.at[j, k], buf_c.at[j, k], c_send.at[j, k], c_recv.at[j, k], "dp", peer)
-
-    def z_copy(k):
-        return remote(zsend.at[k], buf_z.at[k], z_send.at[k], z_recv.at[k], "expert", (my_e + k) % n_e)
-
-    far = [j for j in range(1, half)] + [0]
-    columns = [k for k in range(1, n_e)] + [0]
-    for k in columns:
-        for j in far:
-            s_copy(j, k).start()
-    for k in columns:
-        for j in far:
-            s_copy(j, k).wait_recv()
-            total = part[spot(j, k, core)].astype(jnp.float32) + buf_s[j, k].astype(jnp.float32)
-            acc[j, k] = total.astype(jnp.bfloat16)
-            if j > 0:
-                c_copy(j, k).start()
-    for k in columns:
-        total = acc[0, k].astype(jnp.float32)
-        for j in range(1, half):
-            c_copy(j, k).wait_recv()
-            total = total + buf_c[j, k].astype(jnp.float32)
-        zsend[k] = total.astype(jnp.bfloat16)
-        if k > 0:
-            z_copy(k).start()
-    total = zsend[0].astype(jnp.float32)
-    for k in range(1, n_e):
-        z_copy(k).wait_recv()
-        total = total + buf_z[k].astype(jnp.float32)
-    own = stream[spot(0, 0, core)].astype(jnp.float32)
-    out[...] = (own + total).astype(jnp.bfloat16)
-    for k in range(n_e):
-        for j in range(half):
-            s_copy(j, k).wait_send()
-            if j > 0:
-                c_copy(j, k).wait_send()
-        if k > 0:
-            z_copy(k).wait_send()
-
-
-def sum_and_scatter(part, stream, n, n_e):
-    rows, features = part.shape[0] // n, part.shape[1] // n_e
-    half = n // 2
-    bf16 = jnp.bfloat16
-    dma = pltpu.SemaphoreType.DMA
-    return pl.pallas_call(
-        functools.partial(scatter_kernel, n, n_e),
-        out_shape=jax.ShapeDtypeStruct((rows, features), bf16),
-        in_specs=[whole()] * 2,
-        out_specs=whole(),
-        scratch_shapes=[
+            VMEM((local, per, hidden), bf16),
+            VMEM((local, per, tile), bf16),
+            VMEM((tokens, width), bf16),
             VMEM((half, n_e, rows, features), bf16),
             VMEM((half, n_e, rows, features), bf16),
             VMEM((half, n_e, rows, features), bf16),
             VMEM((n_e, rows, features), bf16),
             VMEM((n_e, rows, features), bf16),
+            VMEM((rows, features), f32),
         ]
         + [dma((half, n_e))] * 4
         + [dma((n_e,))] * 2,
         compiler_params=pltpu.CompilerParams(
-            collective_id=1, has_side_effects=True, vmem_limit_bytes=48 * 2**20
+            dimension_semantics=("arbitrary",), collective_id=1, has_side_effects=True,
+            vmem_limit_bytes=58 * 2**20,
         ),
-        name="sum_scatter",
-    )(part, stream)
+        name="experts_scatter",
+    )(stream, gain, meta, w_gate, w_up, w_down)
 
 
 def body(
@@ -472,10 +496,9 @@
         queries, parent, leaf_ids.reshape(1, -1), routes.T, gate_weights.T, node_of_position.reshape(1, -1),
         cache_keys, cache_values, residual, n, n_e,
     )
-    part = run_experts(
-        stream, norm_gain.reshape(1, -1), meta.reshape(n * rows, 128), w_gate, w_up, w_down, rows
+    layer_out = run_experts(
+        stream, norm_gain.reshape(1, -1), meta.reshape(n * rows, 128), w_gate, w_up, w_down, n, n_e
     )
-    layer_out = sum_and_scatter(part, stream, n, n_e)
     return attention_out, layer_out
 
 

time: 166 us -> 153 us (0.922); the launches traced: 162 us -> 152 us
  Pallas kernels: 156 us -> 147 us
    pallas_call x2 -> x1, Pallas kernels: 93.8 us -> 85.1 us  [run_experts(): pl.pallas_call(functools.partial(expert_kernel, n, n_e, k_steps), grid=(2...]
    unnamed x6 -> x4, local copies, waits for them, and re-layouts: 3.5 us -> 2.23 us
where the time goes in v3:
time: 153 us; the launch traced here: 152 us
  Pallas kernels  147 us (96%)
  local copies, waits for them, and re-layouts  4.85 us (3%)
    pallas_call x1, Pallas kernels, run_experts(): pl.pallas_call(functools.partial(expert_kernel, n, n_e, k_steps), grid=(2...  85.1 us
    pallas_call x1, Pallas kernels, attend_and_gather(): pl.pallas_call(functools.partial(attention_kernel, n, n_e, kv_local, grou...  61.8 us

profile of v3, /device:TPU:24, one launch (start us, length us, event | category | flops | bytes accessed | tf_op | source)
XLA Modules:
  0.0 152.5 jit_solution(5722050489250050770)
XLA Ops:
  0.6 1.3 reshape.17.node
  1.9 1.3 reshape.18.gain
  3.3 61.8 %attention_gather.1 = (bf16[64,1024]{1,0:T(8,128)(2,1)}, bf16[512,4096]{1,0:T(8,128)(2,1)}, bf16[8,64,128]{2,1,0:T(8,128)(2,1)}) custom-call(bf16[64,1024]{1,0:T(8,128)(2,1)} %queries.1, s32[21]{0:T(128)} %parent.1, s32[1,64]{1,0:T(1,128)} %bitcast.6, s32[2,64]{1,0:T(2,128)} %bitcast.5, bf16[2,64]{1,0:T(2,128)(2,1)} %bitcast.7, s32[1,2304]{1,0:T(1,128)} %reshape.17.node, ...), custom_call_target="tpu_custom_call" | custom-call | tf_op jit(solution)/shard_map/attention_gather/pallas_call | solution.py:222
  65.1 0.0 copy-start
  65.1 85.1 %experts_scatter.1 = bf16[64,1024]{1,0:T(8,128)(2,1)} custom-call(bf16[512,4096]{1,0:T(8,128)(2,1)} %get-tuple-element.6.stream, bf16[1,4096]{1,0:T(2,128)(2,1)} %reshape.18.gain, bf16[512,128]{1,0:T(8,128)(2,1)} %bitcast.4, bf16[2,4096,1792]{2,1,0:T(8,128)(2,1)} %w_gate.1, bf16[2,4096,1792]{2,1,0:T(8,128)(2,1)} %w_up.1, bf16[2,1792,4096]{2,1,0:T(8,128)(2,1)} %w_down.1), custom_call_target="tpu_custom_call" | custom-call | tf_op jit(solution)/shard_map/experts_scatter/pallas_call | solution.py:450
  150.3 0.0 copy-done
  150.3 0.7 copy.17
  150.9 1.6 %copy.18 = bf16[64,1024]{1,0:T(8,128)(2,1)} copy(bf16[64,1024]{1,0:T(8,128)(2,1)} %experts_scatter.1) | data formatting | bytes 262144
Async XLA Ops:
  65.1 85.2 %copy-start = (bf16[64,1024]{1,0:T(8,128)(2,1)S(1)}, bf16[64,1024]{1,0:T(8,128)(2,1)}, u32[]{:S(2)}) copy-start(bf16[64,1024]{1,0:T(8,128)(2,1)} %get-tuple-element.10) | copy-start | bytes 393220
